TPU v7x, 512 devices: a whole 4x8x8 slice. The times are simulated.
512 devices in a mesh: brick: 128 (over y, z, core), ch: 4 (over x).
Axes of the slice: x: 4, y: 8, z: 8, core: 2. Of those that a mesh axis runs over, the one named last changes fastest.
Arguments:
- features: bfloat16 [256, 16384], P('ch', 'brick'), may hold values from -6 to 6
- owner_map: int32 [16384, 1], P('brick'), may hold values from 0 to 127; in each aligned block of 128 rows (0 to 127, 128 to 255, ...) at most 2 rows name the same one
- kernel_map: int32 [27, 32768], P(None, 'brick'), may hold values from 0 to 320, as said below
- send_lists: int32 [2, 4096], P(None, 'brick'), may hold values from 0 to 255
- drop_first: int32 [256, 32768], P('ch', 'brick'), may hold values 0 or 1
- drop_second: int32 [256, 32768], P('ch', 'brick'), may hold values 0 or 1
- weight_first: bfloat16 [27, 256, 256], P(None, 'ch'), may hold values from -0.15625 to 0.15625
- weight_second: bfloat16 [27, 256, 256], P(None, 'ch'), may hold values from -0.15625 to 0.15625
- cotangent: bfloat16 [256, 32768], P('ch', 'brick'), may hold values from -24 to 24
Outputs:
- block_out: bfloat16 [256, 32768], P('ch', 'brick')
- grad_features: bfloat16 [256, 16384], P('ch', 'brick')
- grad_weight_first: bfloat16 [27, 256, 256], P(None, 'ch')
- grad_weight_second: bfloat16 [27, 256, 256], P(None, 'ch')
Inputs may be any that keep to these rules, and one draw needn't show every extreme that they name: `owner_map`: among the rows of one scan group, at most 2 are owned by the same brick. `kernel_map`: column 320 means that the neighbour is absent; in the middle offset row, slot i of every brick names column 32 + i.
All inputs are finite; a program needn't handle non-finite values. No bound on the sum of `drop_first` or of `drop_second` on one device may be relied on, other than what follows from the above.
Results may differ from a plain program's by a relative error of at most 0.0064.
Values may be sent and summed in bfloat16 or wider, within the bound.
A program may use at most 64 MiB of HBM per device.

v0:
```python
import jax
import jax.numpy as jnp
from jax import lax
from jax.sharding import PartitionSpec as P

KEEP_RATE = 0.9


def with_halo(block, sides, width):
    for axis, dim in sides:
        count = lax.axis_size(axis)
        forward = [(i, i + 1) for i in range(count - 1)]
        backward = [(target, source) for source, target in forward]
        low = lax.ppermute(
            lax.slice_in_dim(block, block.shape[dim] - width, None, axis=dim), axis, forward
        )
        high = lax.ppermute(lax.slice_in_dim(block, 0, width, axis=dim), axis, backward)
        block = jnp.concatenate([low, block, high], axis=dim)
    return block


def slope_silu(value):
    sig = jax.nn.sigmoid(value)
    return sig * (1.0 + value * (1.0 - sig))


def spread(field, send_lists):
    rim_width = send_lists.shape[1]
    outgoing = jnp.concatenate(
        [jnp.take(field, send_lists[0], axis=1), jnp.take(field, send_lists[1], axis=1)], axis=1
    )
    padded = with_halo(outgoing, (("brick", 1),), rim_width)
    return jnp.concatenate([padded[:, :rim_width], field, padded[:, 3 * rim_width :]], axis=1)


def convolve(extended, kernel_map, weight):
    gathered = jnp.take(extended, kernel_map, axis=1, mode="fill", fill_value=0)
    return (
        lax.psum_scatter(
            jnp.einsum("ckr,kco->or", gathered, weight, preferred_element_type=jnp.float32),
            "ch",
            scatter_dimension=0,
            tiled=True,
        ),
        gathered,
    )


def adjoint(gathered, kernel_map, grad_local, weight, extent):
    gathered_grad = lax.all_gather(grad_local, "ch", axis=0, tiled=True)
    weight_grad = jnp.einsum(
        "ckr,or->kco", gathered, gathered_grad, preferred_element_type=jnp.float32
    )
    pushed = jnp.einsum("kco,or->ckr", weight, gathered_grad, preferred_element_type=jnp.float32)
    returned = (
        jnp.zeros((pushed.shape[0], extent), jnp.float32).at[:, kernel_map].add(pushed, mode="drop")
    )
    return (weight_grad, returned)


def fold_back(returned, send_lists, slot_count):
    rim_width = send_lists.shape[1]
    borders = jnp.concatenate(
        [returned[:, :rim_width], returned[:, rim_width + slot_count :]], axis=1
    )
    padded = with_halo(borders, (("brick", 1),), rim_width)
    interior = returned[:, rim_width : rim_width + slot_count]
    interior = interior.at[:, send_lists[0]].add(padded[:, :rim_width])
    return interior.at[:, send_lists[1]].add(padded[:, 3 * rim_width :])


def local(
    features,
    owner_map,
    kernel_map,
    send_lists,
    drop_first,
    drop_second,
    weight_first,
    weight_second,
    cotangent,
):
    bricks = lax.axis_size("brick")
    channels = features.shape[0]
    slot_count = 2 * features.shape[1]
    capacity = slot_count // bricks
    targets = owner_map[:, 0]
    matches = (targets[:, None] == jnp.arange(bricks, dtype=jnp.int32)[None, :]).astype(jnp.int32)
    running = jnp.cumsum(matches, axis=0)
    ordinal = jnp.sum((running - 1) * matches, axis=1)
    columns = targets * capacity + ordinal
    outgoing = jnp.zeros((channels, slot_count), features.dtype).at[:, columns].set(features)
    tallies = jnp.sum(matches, axis=0)[None, :].astype(jnp.bfloat16)
    arrived, arrived_tallies = (
        lax.all_to_all(
            outgoing.reshape(channels, bricks, capacity),
            "brick",
            split_axis=1,
            concat_axis=1,
            tiled=True,
        ),
        lax.all_to_all(tallies, "brick", split_axis=1, concat_axis=1, tiled=True),
    )
    voxels = arrived.reshape(channels, slot_count)
    occupied = (
        jnp.arange(capacity, dtype=jnp.int32)[None, :]
        < arrived_tallies[0].astype(jnp.int32)[:, None]
    )
    occupied = occupied.reshape(slot_count).astype(jnp.float32)
    keep_first = occupied[None, :] * drop_first.astype(jnp.float32) / KEEP_RATE
    keep_second = occupied[None, :] * drop_second.astype(jnp.float32) / KEEP_RATE
    extended_voxels = spread(voxels, send_lists)
    extent = extended_voxels.shape[1]
    conv_first, gathered_voxels = convolve(extended_voxels, kernel_map, weight_first)
    hidden = (jax.nn.silu(conv_first) * keep_first).astype(jnp.bfloat16)
    extended_hidden = spread(hidden, send_lists)
    conv_second, gathered_hidden = convolve(extended_hidden, kernel_map, weight_second)
    summed = voxels.astype(jnp.float32) + keep_second * conv_second
    block_out = jax.nn.silu(summed).astype(jnp.bfloat16)
    grad_pre = cotangent.astype(jnp.float32) * slope_silu(summed)
    grad_second = (grad_pre * keep_second).astype(jnp.bfloat16)
    weight_grad_second, returned_second = adjoint(
        gathered_hidden, kernel_map, grad_second, weight_second, extent
    )
    grad_hidden = fold_back(returned_second, send_lists, slot_count)
    grad_first = (grad_hidden * keep_first * slope_silu(conv_first)).astype(jnp.bfloat16)
    weight_grad_first, returned_first = adjoint(
        gathered_voxels, kernel_map, grad_first, weight_first, extent
    )
    weight_grad_first, weight_grad_second = lax.psum(
        (weight_grad_first, weight_grad_second), "brick"
    )
    grad_voxels = (grad_pre + fold_back(returned_first, send_lists, slot_count)).astype(
        jnp.bfloat16
    )
    homeward = lax.all_to_all(
        grad_voxels.reshape(channels, bricks, capacity),
        "brick",
        split_axis=1,
        concat_axis=1,
        tiled=True,
    )
    grad_features = jnp.take(homeward.reshape(channels, slot_count), columns, axis=1)
    factor = float(bricks * slot_count) ** (-0.5)
    return (
        block_out,
        grad_features,
        (weight_grad_first * factor).astype(jnp.bfloat16),
        (weight_grad_second * factor).astype(jnp.bfloat16),
    )


def solution(mesh):
    return jax.shard_map(
        local,
        mesh=mesh,
        in_specs=(
            P("ch", "brick"),
            P("brick", None),
            P(None, "brick"),
            P(None, "brick"),
            P("ch", "brick"),
            P("ch", "brick"),
            P(None, "ch", None),
            P(None, "ch", None),
            P("ch", "brick"),
        ),
        out_specs=(P("ch", "brick"), P("ch", "brick"), P(None, "ch", None), P(None, "ch", None)),
        check_vma=False,
    )
```

profile of v0, /device:TPU:24, one launch (start us, length us, event | category | flops | bytes accessed | tf_op | source)
XLA Modules:
  0.0 440.2 jit_solution(2850545359836102251)
XLA Ops:
  13.1 17.3 %all-to-all-start = ((bf16[64,128,2]{0,2,1:T(2,128)(2,1)}), bf16[64,128,2]{0,2,1:T(2,128)(2,1)S(1)}, u32[]{:S(2)}, u32[]{:S(2)}) async-start(bf16[64,128,2]{0,2,1:T(2,128)(2,1)} %bitcast.4), calls=%async_computation | async-start | bytes 131072 | tf_op jit(solution)/shard_map/all_to_all | solution.py:95
  32.9 6.8 %all-to-all-done = bf16[64,128,2]{0,2,1:T(2,128)(2,1)S(1)} async-done(((bf16[64,128,2]{0,2,1:T(2,128)(2,1)}), bf16[64,128,2]{0,2,1:T(2,128)(2,1)S(1)}, u32[]{:S(2)}, u32[]{:S(2)}) %all-to-all-start) | async-done | bytes 32800 | tf_op jit(solution)/shard_map/all_to_all | solution.py:95
  43.0 5.7 %collective-permute-start.1 = (bf16[64,32]{0,1:T(8,128)(2,1)S(1)}, bf16[64,32]{0,1:T(8,128)(2,1)S(1)}, u32[]{:S(2)}, u32[]{:S(2)}) collective-permute-start(bf16[64,32]{0,1:T(8,128)(2,1)S(1)} %select_bitcast_fusion.3), channel_id=1, source_target_pairs={{4,0},{8,4},{12,8},{16,12},{20,16},{24,20},{28,24},{32,28},{36,32}... | collective-permute-start | bytes 12296 | tf_op jit(solution)/shard_map/ppermute | solution.py:17
  50.1 13.0 %gather_fusion.3 = bf16[6912,64]{1,0:T(8,128)(2,1)S(1)} fusion(bf16[64,320]{0,1:T(8,128)(2,1)S(1)} %pad_maximum_fusion, s32[7168]{0:T(1024)S(1)} %pad_clamp_fusion), kind=kCustom, calls=%fused_computation.1.clone | custom fusion | bytes 1797120 | tf_op jit(solution)/shard_map/jit(_take)/gather | solution.py:37
  64.1 2.0 convolution_bitcast_fusion.5
  67.2 19.5 %all_to_all.16 = bf16[1,128,1]{2,0,1:T(2,128)(2,1)S(1)} all-to-all(bf16[1,128,1]{2,0,1:T(2,128)(2,1)S(1)} %copy.100), channel_id=1, replica_groups=mesh['brick'=128,'ch'=4] {'brick'}, dimensions={1} | all-to-all | bytes 512 | tf_op jit(solution)/shard_map/all_to_all | solution.py:102
  86.7 2.4 convert_reduce_fusion
  93.0 1.9 collective-permute-start.2
  95.1 5.8 %collective-permute-start.3 = (bf16[64,32]{1,0:T(8,128)(2,1)S(1)}, bf16[64,32]{1,0:T(8,128)(2,1)S(1)}, u32[]{:S(2)}, u32[]{:S(2)}) collective-permute-start(bf16[64,32]{1,0:T(8,128)(2,1)S(1)} %select_bitcast_fusion.1), channel_id=1, source_target_pairs={{4,0},{8,4},{12,8},{16,12},{20,16},{24,20},{28,24},{32,28},{36,32}... | collective-permute-start | bytes 12296 | tf_op jit(solution)/shard_map/ppermute | solution.py:17
  102.5 13.0 %gather_fusion.6 = bf16[6912,64]{1,0:T(8,128)(2,1)S(1)} fusion(bf16[64,320]{0,1:T(8,128)(2,1)S(1)} %copy.108, s32[7168]{0:T(1024)S(1)} %copy-done.7), kind=kCustom, calls=%fused_computation.5.clone | custom fusion | bytes 1797120 | tf_op jit(solution)/shard_map/jit(_take)/gather | solution.py:37
  118.5 24.4 %reduce-scatter.9.cloned.1.call-done = f32[64,256]{1,0:T(8,128)} async-done(((f32[256,256]{1,0:T(8,128)}), f32[64,256]{1,0:T(8,128)}) %reduce-scatter.9.cloned.1.call-update) | async-done | bytes 65552 | tf_op jit(solution)/shard_map/reduce_scatter | solution.py:39
  143.9 12.2 %all_gather.6 = bf16[256,256]{1,0:T(8,128)(2,1)S(1)} all-gather(bf16[64,256]{1,0:T(8,128)(2,1)S(1)} %multiply_convert_fusion.3), channel_id=1, replica_groups=mesh['brick'=128,'ch'=4] {'ch'}, dimensions={0}, use_global_device_ids=true | all-gather | bytes 163840 | tf_op jit(solution)/shard_map/all_gather | solution.py:50
  157.1 2.5 copy.120
  159.6 39.1 %scatter_custom_fusion.1 = f32[64,320]{0,1:T(8,128)S(1)} fusion(s32[6912]{0:T(1024)} %copy-done.18, f32[6912,64]{1,0:T(8,128)} %bitcast.101, f32[]{:T(128)} %constant.44.clone.1), kind=kCustom, calls=%fused_computation.40 | custom fusion | flops 442368 | bytes 82432 | tf_op jit(solution)/shard_map/scatter-add | solution.py:56
  200.6 5.9 %collective-permute-start.5 = (f32[64,32]{0,1:T(8,128)S(1)}, f32[64,32]{0,1:T(8,128)S(1)}, u32[]{:S(2)}, u32[]{:S(2)}) collective-permute-start(f32[64,32]{0,1:T(8,128)S(1)} %get-tuple-element.44), channel_id=1, source_target_pairs={{4,0},{8,4},{12,8},{16,12},{20,16},{24,20},{28,24},{32,28},{36,32}... | collective-permute-start | bytes 24584 | tf_op jit(solution)/shard_map/ppermute | solution.py:17
  206.5 2.6 convolution_bitcast_fusion
  211.0 12.0 %all_gather.7 = bf16[256,256]{1,0:T(8,128)(2,1)S(1)} all-gather(bf16[64,256]{1,0:T(8,128)(2,1)S(1)} %multiply_convert_fusion.2), channel_id=1, replica_groups=mesh['brick'=128,'ch'=4] {'ch'}, dimensions={0}, use_global_device_ids=true | all-gather | bytes 163840 | tf_op jit(solution)/shard_map/all_gather | solution.py:50
  226.3 2.5 copy.121
  228.8 39.1 %scatter_custom_fusion.4 = f32[64,320]{0,1:T(8,128)S(1)} fusion(s32[6912]{0:T(1024)} %copy-done.18, f32[6912,64]{1,0:T(8,128)} %bitcast.100, f32[]{:T(128)} %constant.44.clone.1), kind=kCustom, calls=%fused_computation.38 | custom fusion | flops 442368 | bytes 82432 | tf_op jit(solution)/shard_map/scatter-add | solution.py:56
  269.9 5.8 %collective-permute-start.7 = (f32[64,32]{0,1:T(8,128)S(1)}, f32[64,32]{0,1:T(8,128)S(1)}, u32[]{:S(2)}, u32[]{:S(2)}) collective-permute-start(f32[64,32]{0,1:T(8,128)S(1)} %get-tuple-element.42), channel_id=1, source_target_pairs={{4,0},{8,4},{12,8},{16,12},{20,16},{24,20},{28,24},{32,28},{36,32}... | collective-permute-start | bytes 24584 | tf_op jit(solution)/shard_map/ppermute | solution.py:17
  278.9 13.2 %all-to-all-start.2 = ((bf16[64,128,2]{0,2,1:T(2,128)(2,1)}), bf16[64,128,2]{0,2,1:T(2,128)(2,1)S(1)}, u32[]{:S(2)}, u32[]{:S(2)}) async-start(bf16[64,128,2]{0,2,1:T(2,128)(2,1)} %bitcast.36), calls=%async_computation.2 | async-start | bytes 131072 | tf_op jit(solution)/shard_map/all_to_all | solution.py:136
  292.2 9.2 %all-to-all-done.2 = bf16[64,128,2]{0,2,1:T(2,128)(2,1)S(1)} async-done(((bf16[64,128,2]{0,2,1:T(2,128)(2,1)}), bf16[64,128,2]{0,2,1:T(2,128)(2,1)S(1)}, u32[]{:S(2)}, u32[]{:S(2)}) %all-to-all-start.2) | async-done | bytes 32800 | tf_op jit(solution)/shard_map/all_to_all | solution.py:136
  302.9 127.1 %all-reduce.3.cloned.1.call-done = (f32[27,64,256]{2,1,0:T(8,128)}, f32[27,64,256]{2,1,0:T(8,128)}) async-done(((f32[27,64,256]{2,1,0:T(8,128)}, f32[27,64,256]{2,1,0:T(8,128)}), (f32[27,64,256]{2,1,0:T(8,128)}, f32[27,64,256]{2,1,0:T(8,128)})) %all-reduce.3.cloned.1.call-update) | async-done | bytes 3538960 | tf_op jit(solution)/shard_map/psum | solution.py:130
  429.9 3.7 multiply_convert_fusion
  (137 shorter events, 39.1 us)
Async XLA Ops:
  7.2 109.3 %copy-start = (bf16[27,64,256]{2,1,0:T(8,128)(2,1)S(1)}, bf16[27,64,256]{2,1,0:T(8,128)(2,1)}, u32[]{:S(2)}) copy-start(bf16[27,64,256]{2,1,0:T(8,128)(2,1)} %param.20) | copy-start | bytes 2654212
  13.1 26.6 %all-to-all-start = ((bf16[64,128,2]{0,2,1:T(2,128)(2,1)}), bf16[64,128,2]{0,2,1:T(2,128)(2,1)S(1)}, u32[]{:S(2)}, u32[]{:S(2)}) async-start(bf16[64,128,2]{0,2,1:T(2,128)(2,1)} %bitcast.4), calls=%async_computation | async-start | bytes 131072 | tf_op jit(solution)/shard_map/all_to_all | solution.py:95
  30.5 60.1 %reduce-scatter.7.cloned.1.call-start = ((), (), s32[]{:S(2)}) async-start(), calls=%async_computation.5 | async-start | bytes 327680 | tf_op jit(solution)/shard_map/reduce_scatter | solution.py:39
  32.9 30.3 %copy-start.19 = (s32[1024]{0:T(1024)}, s32[1024]{0:T(1024)S(1)}, u32[]{:S(2)}) copy-start(s32[1024]{0:T(1024)S(1)} %pad_clamp_fusion.2) | copy-start | bytes 12292
  40.4 8.4 %collective-permute-start = (bf16[64,32]{0,1:T(8,128)(2,1)S(1)}, bf16[64,32]{0,1:T(8,128)(2,1)S(1)}, u32[]{:S(2)}, u32[]{:S(2)}) collective-permute-start(bf16[64,32]{0,1:T(8,128)(2,1)S(1)} %select_bitcast_fusion.4), channel_id=1, source_target_pairs={{0,4},{4,8},{8,12},{12,16},{16,20},{20,24},{24,28},{28,32},{32,36}... | collective-permute-start | bytes 12296 | tf_op jit(solution)/shard_map/ppermute | solution.py:14
  43.0 7.1 %collective-permute-start.1 = (bf16[64,32]{0,1:T(8,128)(2,1)S(1)}, bf16[64,32]{0,1:T(8,128)(2,1)S(1)}, u32[]{:S(2)}, u32[]{:S(2)}) collective-permute-start(bf16[64,32]{0,1:T(8,128)(2,1)S(1)} %select_bitcast_fusion.3), channel_id=1, source_target_pairs={{4,0},{8,4},{12,8},{16,12},{20,16},{24,20},{28,24},{32,28},{36,32}... | collective-permute-start | bytes 12296 | tf_op jit(solution)/shard_map/ppermute | solution.py:17
  66.1 26.9 %copy-start.23 = (pred[32]{0:T(512)(128)(4,1)S(1)}, pred[32]{0:T(512)(128)(4,1)}, u32[]{:S(2)}) copy-start(pred[32]{0:T(512)(128)(4,1)} %copy-done.22) | copy-start | bytes 100
  66.1 29.0 %copy-start.21 = (pred[32]{0:T(512)(128)(4,1)S(1)}, pred[32]{0:T(512)(128)(4,1)}, u32[]{:S(2)}) copy-start(pred[32]{0:T(512)(128)(4,1)} %copy-done.20) | copy-start | bytes 100
  66.1 36.4 %copy-start.7 = (s32[7168]{0:T(1024)S(1)}, s32[7168]{0:T(1024)}, u32[]{:S(2)}) copy-start(s32[7168]{0:T(1024)} %copy-done.6) | copy-start | bytes 86020
  67.0 76.0 %reduce-scatter.9.cloned.1.call-start = ((), (), s32[]{:S(2)}) async-start(), calls=%async_computation.6 | async-start | bytes 327680 | tf_op jit(solution)/shard_map/reduce_scatter | solution.py:39
  93.0 7.8 %collective-permute-start.2 = (bf16[64,32]{1,0:T(8,128)(2,1)S(1)}, bf16[64,32]{1,0:T(8,128)(2,1)S(1)}, u32[]{:S(2)}, u32[]{:S(2)}) collective-permute-start(bf16[64,32]{1,0:T(8,128)(2,1)S(1)} %select_bitcast_fusion.2), channel_id=1, source_target_pairs={{0,4},{4,8},{8,12},{12,16},{16,20},{20,24},{24,28},{28,32},{32,36}... | collective-permute-start | bytes 12296 | tf_op jit(solution)/shard_map/ppermute | solution.py:14
  95.1 7.2 %collective-permute-start.3 = (bf16[64,32]{1,0:T(8,128)(2,1)S(1)}, bf16[64,32]{1,0:T(8,128)(2,1)S(1)}, u32[]{:S(2)}, u32[]{:S(2)}) collective-permute-start(bf16[64,32]{1,0:T(8,128)(2,1)S(1)} %select_bitcast_fusion.1), channel_id=1, source_target_pairs={{4,0},{8,4},{12,8},{16,12},{20,16},{24,20},{28,24},{32,28},{36,32}... | collective-permute-start | bytes 12296 | tf_op jit(solution)/shard_map/ppermute | solution.py:17
  117.8 312.1 %all-reduce.3.cloned.1.call-start = ((), (), s32[]{:S(2)}) async-start(), calls=%async_computation.7 | async-start | bytes 7077888 | tf_op jit(solution)/shard_map/psum | solution.py:130
  198.7 10.4 %collective-permute-start.4 = (f32[64,32]{0,1:T(8,128)S(1)}, f32[64,32]{0,1:T(8,128)S(1)}, u32[]{:S(2)}, u32[]{:S(2)}) collective-permute-start(f32[64,32]{0,1:T(8,128)S(1)} %get-tuple-element.45), channel_id=1, source_target_pairs={{0,4},{4,8},{8,12},{12,16},{16,20},{20,24},{24,28},{28,32},{32,36}... | collective-permute-start | bytes 24584 | tf_op jit(solution)/shard_map/ppermute | solution.py:14
  200.6 9.4 %collective-permute-start.5 = (f32[64,32]{0,1:T(8,128)S(1)}, f32[64,32]{0,1:T(8,128)S(1)}, u32[]{:S(2)}, u32[]{:S(2)}) collective-permute-start(f32[64,32]{0,1:T(8,128)S(1)} %get-tuple-element.44), channel_id=1, source_target_pairs={{4,0},{8,4},{12,8},{16,12},{20,16},{24,20},{28,24},{32,28},{36,32}... | collective-permute-start | bytes 24584 | tf_op jit(solution)/shard_map/ppermute | solution.py:17
  226.3 49.4 %copy-start.9 = (bf16[64,256]{1,0:T(8,128)(2,1)S(1)}, bf16[64,256]{1,0:T(8,128)(2,1)}, u32[]{:S(2)}) copy-start(bf16[64,256]{1,0:T(8,128)(2,1)} %copy-done.8) | copy-start | bytes 98308
  226.3 49.4 %copy-start.14 = (s32[64,256]{1,0:T(8,128)S(1)}, s32[64,256]{1,0:T(8,128)}, u32[]{:S(2)}) copy-start(s32[64,256]{1,0:T(8,128)} %param.18) | copy-start | bytes 196612
  226.3 49.4 %copy-start.15 = (f32[64,256]{1,0:T(8,128)S(1)}, f32[64,256]{1,0:T(8,128)}, u32[]{:S(2)}) copy-start(f32[64,256]{1,0:T(8,128)} %reduce-scatter.9.cloned.1.call-done) | copy-start | bytes 196612
  226.3 49.4 %copy-start.17 = (bf16[64,256]{1,0:T(8,128)(2,1)S(1)}, bf16[64,256]{1,0:T(8,128)(2,1)}, u32[]{:S(2)}) copy-start(bf16[64,256]{1,0:T(8,128)(2,1)} %param.21) | copy-start | bytes 98308
  228.8 63.4 %copy-start.27 = (s32[128,1]{0,1:T(1,128)S(1)}, s32[128,1]{0,1:T(1,128)}, u32[]{:S(2)}) copy-start(s32[128,1]{0,1:T(1,128)} %copy-done.26) | copy-start | bytes 1540
  228.8 73.3 %copy-start.25 = (pred[128]{0:T(512)(128)(4,1)S(1)}, pred[128]{0:T(512)(128)(4,1)}, u32[]{:S(2)}) copy-start(pred[128]{0:T(512)(128)(4,1)} %get-tuple-element.34) | copy-start | bytes 388
  268.0 8.5 %collective-permute-start.6 = (f32[64,32]{0,1:T(8,128)S(1)}, f32[64,32]{0,1:T(8,128)S(1)}, u32[]{:S(2)}, u32[]{:S(2)}) collective-permute-start(f32[64,32]{0,1:T(8,128)S(1)} %get-tuple-element.43), channel_id=1, source_target_pairs={{0,4},{4,8},{8,12},{12,16},{16,20},{20,24},{24,28},{28,32},{32,36}... | collective-permute-start | bytes 24584 | tf_op jit(solution)/shard_map/ppermute | solution.py:14
  269.9 7.5 %collective-permute-start.7 = (f32[64,32]{0,1:T(8,128)S(1)}, f32[64,32]{0,1:T(8,128)S(1)}, u32[]{:S(2)}, u32[]{:S(2)}) collective-permute-start(f32[64,32]{0,1:T(8,128)S(1)} %get-tuple-element.42), channel_id=1, source_target_pairs={{4,0},{8,4},{12,8},{16,12},{20,16},{24,20},{28,24},{32,28},{36,32}... | collective-permute-start | bytes 24584 | tf_op jit(solution)/shard_map/ppermute | solution.py:17
  278.9 22.4 %all-to-all-start.2 = ((bf16[64,128,2]{0,2,1:T(2,128)(2,1)}), bf16[64,128,2]{0,2,1:T(2,128)(2,1)S(1)}, u32[]{:S(2)}, u32[]{:S(2)}) async-start(bf16[64,128,2]{0,2,1:T(2,128)(2,1)} %bitcast.36), calls=%async_computation.2 | async-start | bytes 131072 | tf_op jit(solution)/shard_map/all_to_all | solution.py:136
  (18 other events, 235.9 us)
Sparse Core Ops, SparseCore 0:
  67.1 23.4 reduce-scatter.6
  117.9 24.9 reduce-scatter.8
  224.8 205.0 all-reduce.2
where the time goes:
time: 441 us; the launch traced here: 440 us
  waiting for transfers between devices  172 us (39%)
  other arithmetic  97.8 us (22%)
  starting transfers between devices  61.5 us (14%)
  blocking collectives  43.7 us (10%)
  local copies, waits for them, and re-layouts  42.5 us (10%)
  between operations  14.5 us (3%)
  matrix products  8.64 us (2%)
    psum x1, waiting for transfers between devices, local(): lax.psum((weight_grad_first, weight_grad_second), 'brick')  127 us
    scatter-add x2, other arithmetic, adjoint(): jnp.zeros((pushed.shape[0], extent), jnp.float32).at[:, kernel_map]  78.2 us
    gather x4, local copies, waits for them, and re-layouts, convolve(): gathered = jnp.take(extended, kernel_map, axis=1, mode='fill', fill_value=0)  27.8 us
    reduce_scatter x2, waiting for transfers between devices, convolve(): lax.psum_scatter(jnp.einsum('ckr,kco->or', gathered, weight, preferred_el...  25.8 us
    all_gather x2, blocking collectives, adjoint(): gathered_grad = lax.all_gather(grad_local, 'ch', axis=0, tiled=True)  24.2 us
    ppermute x4, starting transfers between devices, with_halo(): lax.ppermute(lax.slice_in_dim(block, 0, width, axis=dim), axis, backward)  23.1 us
    all_to_all x1, blocking collectives, local(): lax.all_to_all(tallies, 'brick', split_axis=1, concat_axis=1, tiled=True)  19.5 us
    all_to_all x1, starting transfers between devices, local(): lax.all_to_all(outgoing.reshape(channels, bricks, capacity), 'brick', spl...  17.3 us
  transfers between devices with their start and end apart: 13, of which 7 were waited for; matrix products, arithmetic and copies ran while one was open for 13% of the time, Pallas kernels for 0%

commit v1 on v0

--- a/solution.py
+++ b/solution.py
@@ -47,7 +47,24 @@
 
 
 def adjoint(gathered, kernel_map, grad_local, weight, extent):
-    gathered_grad = lax.all_gather(grad_local, "ch", axis=0, tiled=True)
+    size, index, rows = (lax.axis_size("ch"), lax.axis_index("ch"), grad_local.shape[0])
+    right = [(i_2, (i_2 + 1) % size) for i_2 in range(size)]
+    behind = [(i_2, (i_2 - 1) % size) for i_2 in range(size)]
+    out = jnp.zeros(
+        (*grad_local.shape[:0], size * rows, *grad_local.shape[0 + 1 :]), grad_local.dtype
+    )
+    out = lax.dynamic_update_slice_in_dim(out, grad_local, index * rows, axis=0)
+    from_left = from_right = grad_local
+    half = size // 2
+    for step in range(1, half + 1):
+        from_left = lax.ppermute(from_left, "ch", right)
+        out = lax.dynamic_update_slice_in_dim(out, from_left, (index - step) % size * rows, axis=0)
+        if step < size - half:
+            from_right = lax.ppermute(from_right, "ch", behind)
+            out = lax.dynamic_update_slice_in_dim(
+                out, from_right, (index + step) % size * rows, axis=0
+            )
+    gathered_grad = out
     weight_grad = jnp.einsum(
         "ckr,or->kco", gathered, gathered_grad, preferred_element_type=jnp.float32
     )

time: 441 us -> 448 us (1.016)
  blocking collectives: 43.7 us -> 19.5 us
  starting transfers between devices: 61.5 us -> 79.6 us
  waiting for transfers between devices: 172 us -> 181 us
    all_gather x2 -> x0, blocking collectives: 24.2 us -> none  [adjoint(): gathered_grad = lax.all_gather(grad_local, 'ch', axis=0, tiled=True)]
    ppermute x0 -> x6, starting transfers between devices: none -> 18.1 us  [the longest x2 10.2 us: adjoint(): from_right = lax.ppermute(from_right, 'ch', behind)]
    ppermute x0 -> x6, waiting for transfers between devices: none -> 8.72 us  [the longest x4 8.71 us: adjoint(): from_left = lax.ppermute(from_left, 'ch', right)]
  transfers between devices with their start and end apart: 13 -> 19, of which waited for: 7 -> 10; matrix products, arithmetic and copies ran while one was open for 13% -> 13% of each run, Pallas kernels for 0% -> 0%
where the time goes in v1:
time: 448 us; the launch traced here: 447 us
  waiting for transfers between devices  181 us (40%)
  other arithmetic  98.5 us (22%)
  starting transfers between devices  79.6 us (18%)
  local copies, waits for them, and re-layouts  44.3 us (10%)
  blocking collectives  19.5 us (4%)
  between operations  14.6 us (3%)
  matrix products  9.61 us (2%)
    psum x1, waiting for transfers between devices, local(): lax.psum((weight_grad_first, weight_grad_second), 'brick')  126 us
    scatter-add x2, other arithmetic, adjoint(): jnp.zeros((pushed.shape[0], extent), jnp.float32).at[:, kernel_map]  78.2 us
    gather x4, local copies, waits for them, and re-layouts, convolve(): gathered = jnp.take(extended, kernel_map, axis=1, mode='fill', fill_value=0)  27.8 us
    reduce_scatter x2, waiting for transfers between devices, convolve(): lax.psum_scatter(jnp.einsum('ckr,kco->or', gathered, weight, preferred_el...  26.3 us
    ppermute x4, starting transfers between devices, with_halo(): lax.ppermute(lax.slice_in_dim(block, 0, width, axis=dim), axis, backward)  23 us
    all_to_all x1, blocking collectives, local(): lax.all_to_all(tallies, 'brick', split_axis=1, concat_axis=1, tiled=True)  19.5 us
    all_to_all x1, starting transfers between devices, local(): lax.all_to_all(outgoing.reshape(channels, bricks, capacity), 'brick', spl...  17.3 us
    all_to_all x1, starting transfers between devices, local(): lax.all_to_all(grad_voxels.reshape(channels, bricks, capacity), 'brick',...  13.4 us
  transfers between devices with their start and end apart: 19, of which 10 were waited for; matrix products, arithmetic and copies ran while one was open for 13% of the time, Pallas kernels for 0%

profile of v1, /device:TPU:24, one launch (start us, length us, event | category | flops | bytes accessed | tf_op | source)
XLA Modules:
  0.0 446.9 jit_solution(1759369351440152078)
XLA Ops:
  13.1 17.3 %all-to-all-start = ((bf16[64,128,2]{0,2,1:T(2,128)(2,1)}), bf16[64,128,2]{0,2,1:T(2,128)(2,1)S(1)}, u32[]{:S(2)}, u32[]{:S(2)}) async-start(bf16[64,128,2]{0,2,1:T(2,128)(2,1)} %bitcast.4), calls=%async_computation | async-start | bytes 131072 | tf_op jit(solution)/shard_map/all_to_all | solution.py:112
  32.9 6.8 %all-to-all-done = bf16[64,128,2]{0,2,1:T(2,128)(2,1)S(1)} async-done(((bf16[64,128,2]{0,2,1:T(2,128)(2,1)}), bf16[64,128,2]{0,2,1:T(2,128)(2,1)S(1)}, u32[]{:S(2)}, u32[]{:S(2)}) %all-to-all-start) | async-done | bytes 32800 | tf_op jit(solution)/shard_map/all_to_all | solution.py:112
  42.9 5.7 %collective-permute-start.1 = (bf16[64,32]{0,1:T(8,128)(2,1)S(1)}, bf16[64,32]{0,1:T(8,128)(2,1)S(1)}, u32[]{:S(2)}, u32[]{:S(2)}) collective-permute-start(bf16[64,32]{0,1:T(8,128)(2,1)S(1)} %select_bitcast_fusion.3), channel_id=1, source_target_pairs={{4,0},{8,4},{12,8},{16,12},{20,16},{24,20},{28,24},{32,28},{36,32}... | collective-permute-start | bytes 12296 | tf_op jit(solution)/shard_map/ppermute | solution.py:17
  50.1 13.0 %gather_fusion.3 = bf16[6912,64]{1,0:T(8,128)(2,1)S(1)} fusion(bf16[64,320]{0,1:T(8,128)(2,1)S(1)} %pad_maximum_fusion, s32[7168]{0:T(1024)S(1)} %pad_clamp_fusion), kind=kCustom, calls=%fused_computation.1.clone | custom fusion | bytes 1797120 | tf_op jit(solution)/shard_map/jit(_take)/gather | solution.py:37
  67.2 19.5 %all_to_all.16 = bf16[1,128,1]{2,0,1:T(2,128)(2,1)S(1)} all-to-all(bf16[1,128,1]{2,0,1:T(2,128)(2,1)S(1)} %copy.120), channel_id=1, replica_groups=mesh['brick'=128,'ch'=4] {'brick'}, dimensions={1} | all-to-all | bytes 512 | tf_op jit(solution)/shard_map/all_to_all | solution.py:119
  86.6 2.4 convert_reduce_fusion
  95.0 5.8 %collective-permute-start.3 = (bf16[64,32]{1,0:T(8,128)(2,1)S(1)}, bf16[64,32]{1,0:T(8,128)(2,1)S(1)}, u32[]{:S(2)}, u32[]{:S(2)}) collective-permute-start(bf16[64,32]{1,0:T(8,128)(2,1)S(1)} %select_bitcast_fusion.1), channel_id=1, source_target_pairs={{4,0},{8,4},{12,8},{16,12},{20,16},{24,20},{28,24},{32,28},{36,32}... | collective-permute-start | bytes 12296 | tf_op jit(solution)/shard_map/ppermute | solution.py:17
  102.5 13.0 %gather_fusion.6 = bf16[6912,64]{1,0:T(8,128)(2,1)S(1)} fusion(bf16[64,320]{0,1:T(8,128)(2,1)S(1)} %copy.128, s32[7168]{0:T(1024)S(1)} %copy-done.6), kind=kCustom, calls=%fused_computation.5.clone | custom fusion | bytes 1797120 | tf_op jit(solution)/shard_map/jit(_take)/gather | solution.py:37
  117.9 25.0 %reduce-scatter.9.cloned.1.call-done = f32[64,256]{1,0:T(8,128)} async-done(((f32[256,256]{1,0:T(8,128)}), f32[64,256]{1,0:T(8,128)}) %reduce-scatter.9.cloned.1.call-update) | async-done | bytes 65552 | tf_op jit(solution)/shard_map/reduce_scatter | solution.py:39
  147.1 5.1 %collective-permute-start.5 = (bf16[64,256]{1,0:T(8,128)(2,1)S(1)}, bf16[64,256]{1,0:T(8,128)(2,1)S(1)}, u32[]{:S(2)}, u32[]{:S(2)}) collective-permute-start(bf16[64,256]{1,0:T(8,128)(2,1)S(1)} %get-tuple-element.39), channel_id=1, source_target_pairs={{0,3},{1,0},{2,1},{3,2},{4,7},{5,4},{6,5},{7,6},{8,11},{9,8},{10,9... | collective-permute-start | bytes 98312 | tf_op jit(solution)/shard_map/ppermute | solution.py:63
  155.6 3.7 collective-permute-done.6
  161.2 2.4 copy.140
  163.6 39.1 %scatter_custom_fusion.1 = f32[64,320]{0,1:T(8,128)S(1)} fusion(s32[6912]{0:T(1024)} %copy-done.15, f32[6912,64]{1,0:T(8,128)} %bitcast.101, f32[]{:T(128)} %constant.98.clone.1), kind=kCustom, calls=%fused_computation.40 | custom fusion | flops 442368 | bytes 82432 | tf_op jit(solution)/shard_map/scatter-add | solution.py:73
  204.6 5.8 %collective-permute-start.8 = (f32[64,32]{0,1:T(8,128)S(1)}, f32[64,32]{0,1:T(8,128)S(1)}, u32[]{:S(2)}, u32[]{:S(2)}) collective-permute-start(f32[64,32]{0,1:T(8,128)S(1)} %get-tuple-element.48), channel_id=1, source_target_pairs={{4,0},{8,4},{12,8},{16,12},{20,16},{24,20},{28,24},{32,28},{36,32}... | collective-permute-start | bytes 24584 | tf_op jit(solution)/shard_map/ppermute | solution.py:17
  215.7 2.6 convolution_bitcast_fusion
  218.2 5.1 %collective-permute-start.10 = (bf16[64,256]{1,0:T(8,128)(2,1)S(1)}, bf16[64,256]{1,0:T(8,128)(2,1)S(1)}, u32[]{:S(2)}, u32[]{:S(2)}) collective-permute-start(bf16[64,256]{1,0:T(8,128)(2,1)S(1)} %get-tuple-element.37), channel_id=1, source_target_pairs={{0,3},{1,0},{2,1},{3,2},{4,7},{5,4},{6,5},{7,6},{8,11},{9,8},{10,9... | collective-permute-start | bytes 98312 | tf_op jit(solution)/shard_map/ppermute | solution.py:63
  225.4 5.0 %collective-permute-done.11 = bf16[64,256]{1,0:T(8,128)(2,1)S(1)} collective-permute-done((bf16[64,256]{1,0:T(8,128)(2,1)S(1)}, bf16[64,256]{1,0:T(8,128)(2,1)S(1)}, u32[]{:S(2)}, u32[]{:S(2)}) %collective-permute-start.11) | collective-permute-done | bytes 32800 | tf_op jit(solution)/shard_map/ppermute | solution.py:60
  233.8 2.4 copy.141
  236.2 39.1 %scatter_custom_fusion.4 = f32[64,320]{0,1:T(8,128)S(1)} fusion(s32[6912]{0:T(1024)} %copy-done.15, f32[6912,64]{1,0:T(8,128)} %bitcast.100, f32[]{:T(128)} %constant.98.clone.1), kind=kCustom, calls=%fused_computation.38 | custom fusion | flops 442368 | bytes 82432 | tf_op jit(solution)/shard_map/scatter-add | solution.py:73
  277.3 5.8 %collective-permute-start.13 = (f32[64,32]{0,1:T(8,128)S(1)}, f32[64,32]{0,1:T(8,128)S(1)}, u32[]{:S(2)}, u32[]{:S(2)}) collective-permute-start(f32[64,32]{0,1:T(8,128)S(1)} %get-tuple-element.46), channel_id=1, source_target_pairs={{4,0},{8,4},{12,8},{16,12},{20,16},{24,20},{28,24},{32,28},{36,32}... | collective-permute-start | bytes 24584 | tf_op jit(solution)/shard_map/ppermute | solution.py:17
  286.2 13.4 %all-to-all-start.2 = ((bf16[64,128,2]{0,2,1:T(2,128)(2,1)}), bf16[64,128,2]{0,2,1:T(2,128)(2,1)S(1)}, u32[]{:S(2)}, u32[]{:S(2)}) async-start(bf16[64,128,2]{0,2,1:T(2,128)(2,1)} %bitcast.36), calls=%async_computation.2 | async-start | bytes 131072 | tf_op jit(solution)/shard_map/all_to_all | solution.py:153
  299.6 9.2 %all-to-all-done.2 = bf16[64,128,2]{0,2,1:T(2,128)(2,1)S(1)} async-done(((bf16[64,128,2]{0,2,1:T(2,128)(2,1)}), bf16[64,128,2]{0,2,1:T(2,128)(2,1)S(1)}, u32[]{:S(2)}, u32[]{:S(2)}) %all-to-all-start.2) | async-done | bytes 32800 | tf_op jit(solution)/shard_map/all_to_all | solution.py:153
  310.3 126.4 %all-reduce.3.cloned.1.call-done = (f32[27,64,256]{2,1,0:T(8,128)}, f32[27,64,256]{2,1,0:T(8,128)}) async-done(((f32[27,64,256]{2,1,0:T(8,128)}, f32[27,64,256]{2,1,0:T(8,128)}), (f32[27,64,256]{2,1,0:T(8,128)}, f32[27,64,256]{2,1,0:T(8,128)})) %all-reduce.3.cloned.1.call-update) | async-done | bytes 3538960 | tf_op jit(solution)/shard_map/psum | solution.py:147
  436.7 3.7 multiply_convert_fusion
  (149 shorter events, 55.0 us)
Async XLA Ops:
  7.2 109.2 %copy-start = (bf16[27,64,256]{2,1,0:T(8,128)(2,1)S(1)}, bf16[27,64,256]{2,1,0:T(8,128)(2,1)}, u32[]{:S(2)}) copy-start(bf16[27,64,256]{2,1,0:T(8,128)(2,1)} %param.20) | copy-start | bytes 2654212
  13.1 26.6 %all-to-all-start = ((bf16[64,128,2]{0,2,1:T(2,128)(2,1)}), bf16[64,128,2]{0,2,1:T(2,128)(2,1)S(1)}, u32[]{:S(2)}, u32[]{:S(2)}) async-start(bf16[64,128,2]{0,2,1:T(2,128)(2,1)} %bitcast.4), calls=%async_computation | async-start | bytes 131072 | tf_op jit(solution)/shard_map/all_to_all | solution.py:112
  30.5 60.1 %reduce-scatter.7.cloned.1.call-start = ((), (), s32[]{:S(2)}) async-start(), calls=%async_computation.5 | async-start | bytes 327680 | tf_op jit(solution)/shard_map/reduce_scatter | solution.py:39
  40.3 8.4 %collective-permute-start = (bf16[64,32]{0,1:T(8,128)(2,1)S(1)}, bf16[64,32]{0,1:T(8,128)(2,1)S(1)}, u32[]{:S(2)}, u32[]{:S(2)}) collective-permute-start(bf16[64,32]{0,1:T(8,128)(2,1)S(1)} %select_bitcast_fusion.4), channel_id=1, source_target_pairs={{0,4},{4,8},{8,12},{12,16},{16,20},{20,24},{24,28},{28,32},{32,36}... | collective-permute-start | bytes 12296 | tf_op jit(solution)/shard_map/ppermute | solution.py:14
  42.9 7.1 %collective-permute-start.1 = (bf16[64,32]{0,1:T(8,128)(2,1)S(1)}, bf16[64,32]{0,1:T(8,128)(2,1)S(1)}, u32[]{:S(2)}, u32[]{:S(2)}) collective-permute-start(bf16[64,32]{0,1:T(8,128)(2,1)S(1)} %select_bitcast_fusion.3), channel_id=1, source_target_pairs={{4,0},{8,4},{12,8},{16,12},{20,16},{24,20},{28,24},{32,28},{36,32}... | collective-permute-start | bytes 12296 | tf_op jit(solution)/shard_map/ppermute | solution.py:17
  66.9 76.0 %reduce-scatter.9.cloned.1.call-start = ((), (), s32[]{:S(2)}) async-start(), calls=%async_computation.6 | async-start | bytes 327680 | tf_op jit(solution)/shard_map/reduce_scatter | solution.py:39
  93.0 7.8 %collective-permute-start.2 = (bf16[64,32]{1,0:T(8,128)(2,1)S(1)}, bf16[64,32]{1,0:T(8,128)(2,1)S(1)}, u32[]{:S(2)}, u32[]{:S(2)}) collective-permute-start(bf16[64,32]{1,0:T(8,128)(2,1)S(1)} %select_bitcast_fusion.2), channel_id=1, source_target_pairs={{0,4},{4,8},{8,12},{12,16},{16,20},{20,24},{24,28},{28,32},{32,36}... | collective-permute-start | bytes 12296 | tf_op jit(solution)/shard_map/ppermute | solution.py:14
  95.0 7.2 %collective-permute-start.3 = (bf16[64,32]{1,0:T(8,128)(2,1)S(1)}, bf16[64,32]{1,0:T(8,128)(2,1)S(1)}, u32[]{:S(2)}, u32[]{:S(2)}) collective-permute-start(bf16[64,32]{1,0:T(8,128)(2,1)S(1)} %select_bitcast_fusion.1), channel_id=1, source_target_pairs={{4,0},{8,4},{12,8},{16,12},{20,16},{24,20},{28,24},{32,28},{36,32}... | collective-permute-start | bytes 12296 | tf_op jit(solution)/shard_map/ppermute | solution.py:17
  117.8 318.9 %all-reduce.3.cloned.1.call-start = ((), (), s32[]{:S(2)}) async-start(), calls=%async_computation.7 | async-start | bytes 7077888 | tf_op jit(solution)/shard_map/psum | solution.py:147
  145.1 7.1 %collective-permute-start.4 = (bf16[64,256]{1,0:T(8,128)(2,1)S(1)}, bf16[64,256]{1,0:T(8,128)(2,1)S(1)}, u32[]{:S(2)}, u32[]{:S(2)}) collective-permute-start(bf16[64,256]{1,0:T(8,128)(2,1)S(1)} %get-tuple-element.39), channel_id=1, source_target_pairs={{0,1},{1,2},{2,3},{3,0},{4,5},{5,6},{6,7},{7,4},{8,9},{9,10},{10,1... | collective-permute-start | bytes 98312 | tf_op jit(solution)/shard_map/ppermute | solution.py:60
  147.1 7.9 %collective-permute-start.5 = (bf16[64,256]{1,0:T(8,128)(2,1)S(1)}, bf16[64,256]{1,0:T(8,128)(2,1)S(1)}, u32[]{:S(2)}, u32[]{:S(2)}) collective-permute-start(bf16[64,256]{1,0:T(8,128)(2,1)S(1)} %get-tuple-element.39), channel_id=1, source_target_pairs={{0,3},{1,0},{2,1},{3,2},{4,7},{5,4},{6,5},{7,6},{8,11},{9,8},{10,9... | collective-permute-start | bytes 98312 | tf_op jit(solution)/shard_map/ppermute | solution.py:63
  152.2 7.0 %collective-permute-start.6 = (bf16[64,256]{1,0:T(8,128)(2,1)S(1)}, bf16[64,256]{1,0:T(8,128)(2,1)S(1)}, u32[]{:S(2)}, u32[]{:S(2)}) collective-permute-start(bf16[64,256]{1,0:T(8,128)(2,1)S(1)} %collective-permute-done.4), channel_id=1, source_target_pairs={{0,1},{1,2},{2,3},{3,0},{4,5},{5,6},{6,7},{7,4},{8,9},{9,10},{10,1... | collective-permute-start | bytes 98312 | tf_op jit(solution)/shard_map/ppermute | solution.py:60
  202.7 7.7 %collective-permute-start.7 = (f32[64,32]{0,1:T(8,128)S(1)}, f32[64,32]{0,1:T(8,128)S(1)}, u32[]{:S(2)}, u32[]{:S(2)}) collective-permute-start(f32[64,32]{0,1:T(8,128)S(1)} %get-tuple-element.49), channel_id=1, source_target_pairs={{0,4},{4,8},{8,12},{12,16},{16,20},{20,24},{24,28},{28,32},{32,36}... | collective-permute-start | bytes 24584 | tf_op jit(solution)/shard_map/ppermute | solution.py:14
  204.6 7.2 %collective-permute-start.8 = (f32[64,32]{0,1:T(8,128)S(1)}, f32[64,32]{0,1:T(8,128)S(1)}, u32[]{:S(2)}, u32[]{:S(2)}) collective-permute-start(f32[64,32]{0,1:T(8,128)S(1)} %get-tuple-element.48), channel_id=1, source_target_pairs={{4,0},{8,4},{12,8},{16,12},{20,16},{24,20},{28,24},{32,28},{36,32}... | collective-permute-start | bytes 24584 | tf_op jit(solution)/shard_map/ppermute | solution.py:17
  213.7 9.6 %collective-permute-start.9 = (bf16[64,256]{1,0:T(8,128)(2,1)S(1)}, bf16[64,256]{1,0:T(8,128)(2,1)S(1)}, u32[]{:S(2)}, u32[]{:S(2)}) collective-permute-start(bf16[64,256]{1,0:T(8,128)(2,1)S(1)} %get-tuple-element.37), channel_id=1, source_target_pairs={{0,1},{1,2},{2,3},{3,0},{4,5},{5,6},{6,7},{7,4},{8,9},{9,10},{10,1... | collective-permute-start | bytes 98312 | tf_op jit(solution)/shard_map/ppermute | solution.py:60
  218.2 7.1 %collective-permute-start.10 = (bf16[64,256]{1,0:T(8,128)(2,1)S(1)}, bf16[64,256]{1,0:T(8,128)(2,1)S(1)}, u32[]{:S(2)}, u32[]{:S(2)}) collective-permute-start(bf16[64,256]{1,0:T(8,128)(2,1)S(1)} %get-tuple-element.37), channel_id=1, source_target_pairs={{0,3},{1,0},{2,1},{3,2},{4,7},{5,4},{6,5},{7,6},{8,11},{9,8},{10,9... | collective-permute-start | bytes 98312 | tf_op jit(solution)/shard_map/ppermute | solution.py:63
  223.4 7.0 %collective-permute-start.11 = (bf16[64,256]{1,0:T(8,128)(2,1)S(1)}, bf16[64,256]{1,0:T(8,128)(2,1)S(1)}, u32[]{:S(2)}, u32[]{:S(2)}) collective-permute-start(bf16[64,256]{1,0:T(8,128)(2,1)S(1)} %collective-permute-done.9), channel_id=1, source_target_pairs={{0,1},{1,2},{2,3},{3,0},{4,5},{5,6},{6,7},{7,4},{8,9},{9,10},{10,1... | collective-permute-start | bytes 98312 | tf_op jit(solution)/shard_map/ppermute | solution.py:60
  233.7 49.4 %copy-start.8 = (bf16[64,256]{1,0:T(8,128)(2,1)S(1)}, bf16[64,256]{1,0:T(8,128)(2,1)}, u32[]{:S(2)}) copy-start(bf16[64,256]{1,0:T(8,128)(2,1)} %copy-done.7) | copy-start | bytes 98308
  233.7 49.4 %copy-start.11 = (s32[64,256]{1,0:T(8,128)S(1)}, s32[64,256]{1,0:T(8,128)}, u32[]{:S(2)}) copy-start(s32[64,256]{1,0:T(8,128)} %param.18) | copy-start | bytes 196612
  236.2 63.4 %copy-start.24 = (s32[128,1]{0,1:T(1,128)S(1)}, s32[128,1]{0,1:T(1,128)}, u32[]{:S(2)}) copy-start(s32[128,1]{0,1:T(1,128)} %copy-done.23) | copy-start | bytes 1540
  236.2 73.3 %copy-start.22 = (pred[128]{0:T(512)(128)(4,1)S(1)}, pred[128]{0:T(512)(128)(4,1)}, u32[]{:S(2)}) copy-start(pred[128]{0:T(512)(128)(4,1)} %get-tuple-element.34) | copy-start | bytes 388
  275.4 8.5 %collective-permute-start.12 = (f32[64,32]{0,1:T(8,128)S(1)}, f32[64,32]{0,1:T(8,128)S(1)}, u32[]{:S(2)}, u32[]{:S(2)}) collective-permute-start(f32[64,32]{0,1:T(8,128)S(1)} %get-tuple-element.47), channel_id=1, source_target_pairs={{0,4},{4,8},{8,12},{12,16},{16,20},{20,24},{24,28},{28,32},{32,36}... | collective-permute-start | bytes 24584 | tf_op jit(solution)/shard_map/ppermute | solution.py:14
  277.3 7.4 %collective-permute-start.13 = (f32[64,32]{0,1:T(8,128)S(1)}, f32[64,32]{0,1:T(8,128)S(1)}, u32[]{:S(2)}, u32[]{:S(2)}) collective-permute-start(f32[64,32]{0,1:T(8,128)S(1)} %get-tuple-element.46), channel_id=1, source_target_pairs={{4,0},{8,4},{12,8},{16,12},{20,16},{24,20},{28,24},{32,28},{36,32}... | collective-permute-start | bytes 24584 | tf_op jit(solution)/shard_map/ppermute | solution.py:17
  286.2 22.6 %all-to-all-start.2 = ((bf16[64,128,2]{0,2,1:T(2,128)(2,1)}), bf16[64,128,2]{0,2,1:T(2,128)(2,1)S(1)}, u32[]{:S(2)}, u32[]{:S(2)}) async-start(bf16[64,128,2]{0,2,1:T(2,128)(2,1)} %bitcast.36), calls=%async_computation.2 | async-start | bytes 131072 | tf_op jit(solution)/shard_map/all_to_all | solution.py:153
  (21 other events, 495.7 us)
Sparse Core Ops, SparseCore 0:
  67.1 23.4 reduce-scatter.6
  117.9 24.9 reduce-scatter.8
  232.3 204.3 all-reduce.2
